TPU v7x, 32 devices: a whole 2x2x4 slice. The times are simulated.
32 devices in a mesh: chord: 4 (over y, x), wall: 8 (over z, core).
Axes of the slice: x: 2, y: 2, z: 4, core: 2. Of those that a mesh axis runs over, the one named last changes fastest.
Arguments:
- rhs: float32 [5, 16, 16, 512], P(None, None, 'wall', 'chord'), may hold values from -0.3 to 0.3
- jet_mask: int32 [16, 16, 512], P(None, 'wall', 'chord'), may hold values 0 or 1
- jet_source: float32 [5], replicated, may hold values from -0.3 to 0.3
- wall_flags: int32 [16, 512], P(None, 'chord'), may hold values from 0 to 2
- bc_table: float32 [3, 5], replicated, may hold values from 0.2 to 1.5
- xi_lower: float32 [5, 5, 16, 16, 512], P(None, None, None, 'wall', 'chord'), may hold values from -1.2 to 1.2
- xi_upper: float32 [5, 5, 16, 16, 512], P(None, None, None, 'wall', 'chord'), may hold values from -1.2 to 1.2
- eta_lower: float32 [5, 5, 16, 16, 512], P(None, None, None, 'wall', 'chord'), may hold values from -1.2 to 1.2
- eta_upper: float32 [5, 5, 16, 16, 512], P(None, None, None, 'wall', 'chord'), may hold values from -1.2 to 1.2
Outputs:
- increment: float32 [5, 16, 16, 512], P(None, None, 'wall', 'chord')
All inputs are finite; a program needn't handle non-finite values. No bound on the sum of `jet_mask` on one device may be relied on, other than what follows from the above.
Results may differ from a plain program's by a relative error of at most 0.00019.
Values sent between devices are 32-bit elements; how exact they have to be, the bound alone decides.
A program may use at most 64 MiB of HBM per device.

v0:
```python
import jax
import jax.numpy as jnp
from jax import lax
from jax.sharding import PartitionSpec as P

HIGH = lax.Precision.HIGHEST


def carried_in(part, axis, combine, identity, reverse):
    count = lax.axis_size(axis)
    place = lax.axis_index(axis)
    ahead = count - 1 - place if reverse else place
    gathered = jax.tree.map(lambda a: lax.all_gather(a, axis), part)
    state = jax.tree.map(lambda a, e: jnp.zeros_like(a) + jnp.asarray(e, a.dtype), part, identity)

    def one(hop, state):
        source = count - 1 - hop if reverse else hop
        return combine(
            state, jax.tree.map(lambda a: lax.dynamic_index_in_dim(a, source, 0, False), gathered)
        )

    return lax.fori_loop(0, ahead, one, state)


def block_product(left, right):
    return jnp.sum(left[:, :, None] * right[None, :, :], axis=1)


def compose(earlier, later):
    first_blocks, first_values = earlier
    second_blocks, second_values = later
    blocks = block_product(second_blocks, first_blocks)
    values = block_product(second_blocks, first_values) + second_values
    return (blocks, values)


def prefix_maps(blocks, values, chain_axis, reverse):
    if reverse:
        blocks = jnp.flip(blocks, chain_axis)
        values = jnp.flip(values, chain_axis)
    reach, state = lax.associative_scan(compose, (blocks, values), axis=chain_axis)
    if reverse:
        reach = jnp.flip(reach, chain_axis)
        state = jnp.flip(state, chain_axis)
    return (reach, state)


def identity_of(summary):
    blocks, values = summary
    eye = jnp.eye(5, dtype=jnp.float32).reshape((5, 5) + (1,) * (blocks.ndim - 2))
    return (jnp.broadcast_to(eye, blocks.shape), jnp.zeros_like(values))


def chain_sweep(blocks, values, chain_axis, reverse, carry_fn):
    reach, state = prefix_maps(blocks, values, chain_axis, reverse)
    edge = 0 if reverse else blocks.shape[chain_axis] - 1
    summary = (
        lax.index_in_dim(reach, edge, chain_axis, keepdims=False),
        lax.index_in_dim(state, edge, chain_axis, keepdims=False),
    )
    inflow = carry_fn(summary)[1]
    inflow = jnp.expand_dims(inflow, chain_axis)
    return state + block_product(reach, inflow)


def wall_down(summary):
    return carried_in(summary, "wall", compose, identity_of(summary), False)


def wall_up(summary):
    return carried_in(summary, "wall", compose, identity_of(summary), True)


def per_device(
    rhs, jet_mask, jet_source, wall_flags, bc_table, xi_lower, xi_upper, eta_lower, eta_upper
):
    source = rhs + jet_mask.astype(jnp.float32)[None] * jet_source[:, None, None, None]
    source = source[:, None]
    moved, lower_lines, upper_lines = (
        lax.all_to_all(source, "chord", split_axis=2, concat_axis=4, tiled=True),
        lax.all_to_all(xi_lower, "chord", split_axis=2, concat_axis=4, tiled=True),
        lax.all_to_all(xi_upper, "chord", split_axis=2, concat_axis=4, tiled=True),
    )
    ahead = prefix_maps(lower_lines, moved, 4, False)[1]
    behind = prefix_maps(upper_lines, ahead, 4, True)[1]
    solved = lax.all_to_all(behind, "chord", split_axis=4, concat_axis=2, tiled=True)
    onehot = (
        wall_flags[None] == jnp.arange(bc_table.shape[0], dtype=jnp.int32)[:, None, None]
    ).astype(jnp.float32)
    factor = jnp.einsum("fa,fki->aki", bc_table, onehot, precision=HIGH)
    first_row = (lax.axis_index("wall") == 0) & (jnp.arange(solved.shape[3], dtype=jnp.int32) == 0)
    scaled = (
        jnp.where(
            first_row[None, None, None, :, None], factor[:, None, :, None, :], jnp.float32(1.0)
        )
        * solved
    )
    lifted = chain_sweep(eta_lower, scaled, 3, False, wall_down)
    result = chain_sweep(eta_upper, lifted, 3, True, wall_up)
    return result[:, 0]


def solution(mesh):
    placed = (
        P(None, None, "wall", "chord"),
        P(None, "wall", "chord"),
        P(),
        P(None, "chord"),
        P(),
        P(None, None, None, "wall", "chord"),
        P(None, None, None, "wall", "chord"),
        P(None, None, None, "wall", "chord"),
        P(None, None, None, "wall", "chord"),
    )
    return jax.shard_map(
        per_device,
        mesh=mesh,
        in_specs=placed,
        out_specs=P(None, None, "wall", "chord"),
        check_vma=False,
    )
```

profile of v0, /device:TPU:0, one launch (start us, length us, event | category | flops | bytes accessed | tf_op | source)
XLA Modules:
  0.0 437.4 jit_solution(6902419832157176605)
XLA Ops:
  8.9 5.2 %all-to-all-start = ((f32[5,1,16,2,128]{4,3,0,1,2:T(2,128)}), f32[5,1,16,2,128]{4,3,0,1,2:T(2,128)S(1)}, u32[]{:S(2)}, u32[]{:S(2)}) async-start(f32[5,1,16,2,128]{4,3,0,1,2:T(2,128)} %fusion.10), calls=%async_computation | async-start | bytes 163840 | tf_op jit(solution)/shard_map/all_to_all | solution.py:80
  16.0 3.0 all-to-all-done
  19.0 3.5 all-to-all-start.1
  29.3 4.2 all-to-all-start.2
  33.9 9.2 %slice.490 = f32[5,5,4,2,255]{4,3,2,1,0:T(2,128)S(1)} slice(f32[5,5,4,2,512]{4,3,2,1,0:T(2,128)S(1)} %all_to_all.59), slice={[0:5:1], [0:5:1], [0:4:1], [0:2:1], [2:512:2]} | slice | bytes 408000 | tf_op jit(solution)/shard_map/slice | solution.py:41
  43.1 9.1 %slice.491 = f32[5,5,4,2,256]{4,3,2,1,0:T(2,128)S(1)} slice(f32[5,5,4,2,512]{4,3,2,1,0:T(2,128)S(1)} %all_to_all.59), slice={[0:5:1], [0:5:1], [0:4:1], [0:2:1], [1:512:2]} | slice | bytes 409600 | tf_op jit(solution)/shard_map/slice | solution.py:41
  52.2 9.1 %slice.495 = f32[5,5,4,2,256]{4,3,2,1,0:T(2,128)S(1)} slice(f32[5,5,4,2,512]{4,3,2,1,0:T(2,128)S(1)} %all_to_all.59), slice={[0:5:1], [0:5:1], [0:4:1], [0:2:1], [0:511:2]} | slice | bytes 409600 | tf_op jit(solution)/shard_map/slice | solution.py:41
  64.1 5.6 %slice.497 = f32[5,5,4,2,128]{4,2,3,1,0:T(4,128)S(1)} slice(f32[5,5,4,2,256]{4,2,3,1,0:T(4,128)S(1)} %multiply_reduce_fusion.3), slice={[0:5:1], [0:5:1], [0:4:1], [0:2:1], [1:256:2]} | slice | bytes 204800 | tf_op jit(solution)/shard_map/slice | solution.py:41
  69.7 5.6 %slice.501 = f32[5,5,4,2,128]{4,2,3,1,0:T(4,128)S(1)} slice(f32[5,5,4,2,256]{4,2,3,1,0:T(4,128)S(1)} %multiply_reduce_fusion.3), slice={[0:5:1], [0:5:1], [0:4:1], [0:2:1], [0:255:2]} | slice | bytes 204800 | tf_op jit(solution)/shard_map/slice | solution.py:41
  77.2 3.9 slice.502
  81.1 3.9 slice.503
  85.8 3.9 slice.507
  91.2 3.0 slice.509
  94.3 3.0 slice.513
  97.5 2.6 slice.514
  100.1 2.6 slice.519
  102.7 2.6 slice.515
  105.5 2.4 slice.525
  107.9 2.4 slice.521
  130.8 2.4 slice.520
  141.4 3.0 slice.508
  148.6 2.3 pad.151
  151.1 2.3 pad.150
  154.5 5.5 %slice.496 = f32[5,5,4,2,127]{4,2,3,1,0:T(4,128)S(1)} slice(f32[5,5,4,2,256]{4,2,3,1,0:T(4,128)S(1)} %multiply_reduce_fusion.3), slice={[0:5:1], [0:5:1], [0:4:1], [0:2:1], [2:256:2]} | slice | bytes 203200 | tf_op jit(solution)/shard_map/slice | solution.py:41
  160.3 2.9 pad.152
  163.2 3.0 pad.153
  166.2 4.3 pad.155
  170.7 4.3 pad.154
  175.3 4.3 pad.156
  179.6 4.3 pad.157
  188.1 9.1 %slice.559 = f32[5,5,4,2,256]{4,3,2,1,0:T(2,128)S(1)} slice(f32[5,5,4,2,512]{4,3,2,1,0:T(2,128)S(1)} %all_to_all.63), slice={[0:5:1], [0:5:1], [0:4:1], [0:2:1], [0:511:2]} | slice | bytes 409600 | tf_op jit(solution)/shard_map/slice | solution.py:41
  197.2 9.1 %slice.566 = f32[5,5,4,2,256]{4,3,2,1,0:T(2,128)S(1)} slice(f32[5,5,4,2,512]{4,3,2,1,0:T(2,128)S(1)} %all_to_all.63), slice={[0:5:1], [0:5:1], [0:4:1], [0:2:1], [1:512:2]} | slice | bytes 409600 | tf_op jit(solution)/shard_map/slice | solution.py:41
  211.2 5.6 %slice.569 = f32[5,5,4,2,128]{4,2,3,1,0:T(4,128)S(1)} slice(f32[5,5,4,2,256]{4,2,3,1,0:T(4,128)S(1)} %multiply_reduce_fusion.2), slice={[0:5:1], [0:5:1], [0:4:1], [0:2:1], [1:256:2]} | slice | bytes 204800 | tf_op jit(solution)/shard_map/slice | solution.py:41
  216.7 5.6 %slice.573 = f32[5,5,4,2,128]{4,2,3,1,0:T(4,128)S(1)} slice(f32[5,5,4,2,256]{4,2,3,1,0:T(4,128)S(1)} %multiply_reduce_fusion.2), slice={[0:5:1], [0:5:1], [0:4:1], [0:2:1], [0:255:2]} | slice | bytes 204800 | tf_op jit(solution)/shard_map/slice | solution.py:41
  224.2 3.9 slice.574
  228.1 3.9 slice.575
  232.8 3.9 slice.579
  238.3 3.0 slice.581
  241.3 3.0 slice.585
  244.5 2.6 slice.586
  247.2 2.6 slice.591
  249.8 2.6 slice.587
  252.6 2.4 slice.597
  254.9 2.4 slice.593
  277.8 2.4 slice.592
  288.5 3.0 slice.580
  295.6 2.3 pad.169
  301.6 5.5 %slice.568 = f32[5,5,4,2,127]{4,2,3,1,0:T(4,128)S(1)} slice(f32[5,5,4,2,256]{4,2,3,1,0:T(4,128)S(1)} %multiply_reduce_fusion.2), slice={[0:5:1], [0:5:1], [0:4:1], [0:2:1], [2:256:2]} | slice | bytes 203200 | tf_op jit(solution)/shard_map/slice | solution.py:41
  307.3 2.9 pad.170
  310.2 3.0 pad.171
  313.3 9.1 %slice.557 = f32[5,5,4,2,255]{4,3,2,1,0:T(2,128)S(1)} slice(f32[5,5,4,2,512]{4,3,2,1,0:T(2,128)S(1)} %all_to_all.63), slice={[0:5:1], [0:5:1], [0:4:1], [0:2:1], [1:510:2]} | slice | bytes 408000 | tf_op jit(solution)/shard_map/slice | solution.py:41
  324.4 4.3 pad.173
  328.8 4.3 pad.172
  334.6 4.3 pad.174
  338.9 4.3 pad.175
  345.2 2.9 reshape.385
  348.1 4.2 all-to-all-start.3
  352.3 4.9 %all-to-all-done.3 = f32[4,1,5120]{2,1,0:T(1,128)S(1)} async-done(((f32[4,1,5120]{2,1,0:T(1,128)}), f32[4,1,5120]{2,1,0:T(1,128)S(1)}, u32[]{:S(2)}, u32[]{:S(2)}) %all-to-all-start.3) | async-done | bytes 81952 | tf_op jit(solution)/shard_map/all_to_all | solution.py:86
  358.5 2.5 reshape.386
  363.6 15.1 %all-gather.1 = f32[40,1,16,1,128]{4,2,3,1,0:T(8,128)S(1)} all-gather(f32[5,1,16,1,128]{4,2,3,1,0:T(8,128)S(1)} %fusion.12), channel_id=3, replica_groups=mesh['chord'=4,'wall'=8] {'wall'}, dimensions={0}, use_global_device_ids=true | all-gather | bytes 368640 | tf_op jit(solution)/shard_map/all_gather | solution.py:13
  378.7 10.8 %all-gather.7.cloned.1.call-done = f32[40,5,16,1,128]{4,2,3,1,0:T(8,128)} async-done(((f32[5,5,16,1,128]{4,2,3,1,0:T(8,128)}), f32[40,5,16,1,128]{4,2,3,1,0:T(8,128)}) %all-gather.7.cloned.1.call-update) | async-done | bytes 1638416 | tf_op jit(solution)/shard_map/all_gather | solution.py:13
  391.0 20.1 %all-gather.3 = f32[40,1,16,1,128]{4,2,3,1,0:T(8,128)S(1)} all-gather(f32[5,1,16,1,128]{4,2,3,1,0:T(8,128)S(1)} %fusion.14), channel_id=5, replica_groups=mesh['chord'=4,'wall'=8] {'wall'}, dimensions={0}, use_global_device_ids=true | all-gather | bytes 368640 | tf_op jit(solution)/shard_map/all_gather | solution.py:13
  411.1 11.8 %all-gather.9.cloned.1.call-done = f32[40,5,16,1,128]{4,2,3,1,0:T(8,128)} async-done(((f32[5,5,16,1,128]{4,2,3,1,0:T(8,128)}), f32[40,5,16,1,128]{4,2,3,1,0:T(8,128)}) %all-gather.9.cloned.1.call-update) | async-done | bytes 1638416 | tf_op jit(solution)/shard_map/all_gather | solution.py:13
  422.9 7.0 %while.27 = (s32[]{:T(128)}, f32[5,1,16,128]{3,2,0,1:T(8,128)S(1)}, s32[]{:T(128)}, f32[8,5,5,16,128]{4,3,2,1,0:T(8,128)}, f32[8,5,1,16,128]{4,3,2,1,0:T(8,128)S...) while((s32[]{:T(128)}, f32[5,1,16,128]{3,2,0,1:T(8,128)S(1)}, s32[]{:T(128)}, ...), condition=%wide.region_60.61_spmd, body=%wide.region_58.60_spmd.sunk | while | flops 102406 | bytes 409755 | solution.py:22
  (349 shorter events, 121.2 us)
Async XLA Ops:
  6.5 16.8 %copy-start = (f32[3,5]{1,0:T(4,128)S(1)}, f32[3,5]{1,0:T(4,128)}, u32[]{:S(2)}) copy-start(f32[3,5]{1,0:T(4,128)} %param.17) | copy-start | bytes 184
  6.5 15.9 %copy-start.4 = (f32[5,5,16,2,128]{4,3,2,1,0:T(2,128)S(1)}, f32[5,5,16,2,128]{4,3,2,1,0:T(2,128)}, u32[]{:S(2)}) copy-start(f32[5,5,16,2,128]{4,3,2,1,0:T(2,128)} %param.19) | copy-start | bytes 1228804
  6.5 16.8 %copy-start.5 = (s32[16,128]{1,0:T(8,128)S(1)}, s32[16,128]{1,0:T(8,128)}, u32[]{:S(2)}) copy-start(s32[16,128]{1,0:T(8,128)} %param.16) | copy-start | bytes 24580
  8.9 10.1 %all-to-all-start = ((f32[5,1,16,2,128]{4,3,0,1,2:T(2,128)}), f32[5,1,16,2,128]{4,3,0,1,2:T(2,128)S(1)}, u32[]{:S(2)}, u32[]{:S(2)}) async-start(f32[5,1,16,2,128]{4,3,0,1,2:T(2,128)} %fusion.10), calls=%async_computation | async-start | bytes 163840 | tf_op jit(solution)/shard_map/all_to_all | solution.py:80
  19.0 10.3 %all-to-all-start.1 = ((f32[5,5,16,2,128]{4,3,1,0,2:T(2,128)}), f32[5,5,16,2,128]{4,3,1,0,2:T(2,128)S(1)}, u32[]{:S(2)}, u32[]{:S(2)}) async-start(f32[5,5,16,2,128]{4,3,1,0,2:T(2,128)} %copy.343), calls=%async_computation.1 | async-start | bytes 819200 | tf_op jit(solution)/shard_map/all_to_all | solution.py:81
  23.7 28.5 %copy-start.1 = (f32[5,1,4,2,512]{4,3,2,0,1:T(2,128)}, f32[5,1,4,2,512]{4,3,2,0,1:T(2,128)S(1)}, u32[]{:S(2)}) copy-start(f32[5,1,4,2,512]{4,3,2,0,1:T(2,128)S(1)} %all_to_all.55) | copy-start | bytes 245764
  29.3 158.4 %all-to-all-start.2 = ((f32[5,5,16,2,128]{4,3,1,0,2:T(2,128)}), f32[5,5,16,2,128]{4,3,1,0,2:T(2,128)S(1)}, u32[]{:S(2)}, u32[]{:S(2)}) async-start(f32[5,5,16,2,128]{4,3,1,0,2:T(2,128)} %copy.391), calls=%async_computation.2 | async-start | bytes 819200 | tf_op jit(solution)/shard_map/all_to_all | solution.py:82
  140.7 34.5 %slice-start = ((f32[5,1,4,2,512]{4,3,2,0,1:T(2,128)}), f32[5,1,4,2,1]{4,3,2,0,1:T(2,128)S(1)}, s32[]{:S(2)}) async-start(f32[5,1,4,2,512]{4,3,2,0,1:T(2,128)} %copy-done.1), calls=%async_computation.6 | async-start | bytes 40960 | tf_op jit(solution)/shard_map/slice | solution.py:41
  348.1 9.1 %all-to-all-start.3 = ((f32[4,1,5120]{2,1,0:T(1,128)}), f32[4,1,5120]{2,1,0:T(1,128)S(1)}, u32[]{:S(2)}, u32[]{:S(2)}) async-start(f32[4,1,5120]{2,1,0:T(1,128)} %reshape.385), calls=%async_computation.3 | async-start | bytes 163840 | tf_op jit(solution)/shard_map/all_to_all | solution.py:86
  352.3 37.2 %all-gather.7.cloned.1.call-start = ((), (), s32[]{:S(2)}) async-start(), calls=%async_computation.4 | async-start | bytes 1843200 | tf_op jit(solution)/shard_map/all_gather | solution.py:13
  361.1 1.2 copy-start.2
  363.5 59.3 %all-gather.9.cloned.1.call-start = ((), (), s32[]{:S(2)}) async-start(), calls=%async_computation.5 | async-start | bytes 1843200 | tf_op jit(solution)/shard_map/all_gather | solution.py:13
  378.7 10.9 %copy-start.3 = (f32[5,5,16,2,128]{4,3,2,1,0:T(2,128)S(1)}, f32[5,5,16,2,128]{4,3,2,1,0:T(2,128)}, u32[]{:S(2)}) copy-start(f32[5,5,16,2,128]{4,3,2,1,0:T(2,128)} %param.21) | copy-start | bytes 1228804
Sparse Core Ops, SparseCore 0:
  363.7 25.8 all-gather.6
  391.2 31.6 all-gather.8
where the time goes:
time: 438 us; the launch traced here: 437 us
  local copies, waits for them, and re-layouts  317 us (72%)
  blocking collectives  35.2 us (8%)
  waiting for transfers between devices  30.5 us (7%)
  other arithmetic  21.8 us (5%)
  starting transfers between devices  17 us (4%)
  between operations  15.4 us (4%)
    slice x117, local copies, waits for them, and re-layouts, prefix_maps(): lax.associative_scan(compose, (blocks, values), axis=chain_axis)  217 us
    pad x32, local copies, waits for them, and re-layouts, prefix_maps(): lax.associative_scan(compose, (blocks, values), axis=chain_axis)  83.2 us
    all_gather x2, blocking collectives, carried_in(): gathered = jax.tree.map(lambda a: lax.all_gather(a, axis), part)  35.2 us
    all_gather x2, waiting for transfers between devices, carried_in(): gathered = jax.tree.map(lambda a: lax.all_gather(a, axis), part)  22.6 us
    reduce_sum x62, other arithmetic, block_product(): return jnp.sum(left[:, :, None] * right[None, :, :], axis=1)  12.7 us
    unnamed x24, local copies, waits for them, and re-layouts  9.97 us
  transfers between devices with their start and end apart: 6, of which 4 were waited for; matrix products, arithmetic and copies ran while one was open for 37% of the time, Pallas kernels for 0%

commit v1 on v0

v1 whole, which is shorter than its diff:
```python
import functools

import jax
import jax.numpy as jnp
from jax import lax
from jax.experimental import pallas as pl
from jax.experimental.pallas import tpu as pltpu
from jax.sharding import PartitionSpec as P

C = 5
ROWS = 8


def shifted(x, step, fill_eye, reverse):
    a, m, rows, width = x.shape
    flat = x.reshape(a * m * rows, width)
    moved = pltpu.roll(flat, width - step if reverse else step, 1).reshape(x.shape)
    lane = lax.broadcasted_iota(jnp.int32, x.shape, 3)
    keep = lane < width - step if reverse else lane >= step
    row = lax.broadcasted_iota(jnp.int32, x.shape, 0)
    col = lax.broadcasted_iota(jnp.int32, x.shape, 1)
    fill = jnp.where(row == col, 1.0, 0.0).astype(jnp.float32)
    return jnp.where(keep, moved, fill)


def apply_blocks(left, right):
    total = left[:, 0:1] * right[0:1]
    for b in range(1, C):
        total = total + left[:, b : b + 1] * right[b : b + 1]
    return total


def scan_lanes(blocks, values, reverse):
    both = jnp.concatenate([blocks, values], axis=1)
    step = 1
    while step < both.shape[3]:
        moved = shifted(both, step, True, reverse)
        made = apply_blocks(both[:, :C], moved)
        both = jnp.concatenate([made[:, :C], made[:, C:] + both[:, C:]], axis=1)
        step *= 2
    return both


def kernel(
    n_chord, n_wall, n_own,
    rhs_h, mask_h, jet, flags_v, table, xl_h, xu_h, el_h, eu_h,
    out_h,
    rhs, mask, xl, xu, el, eu, prefix, summary, sol, sol_in, res,
    load_sem, own_sem, chord_send, chord_recv, el_send, el_recv, eu_send, eu_recv,
    sol_send, sol_recv, res_send, res_recv,
):
    chord = lax.axis_index("chord")
    wall = lax.axis_index("wall")
    rows_per_owner = sol.shape[2]
    kpo = rows_per_owner // 2
    groups = rhs.shape[1] // ROWS
    width = rhs.shape[2]

    def when(own, cond_of):
        if n_own == n_wall:
            own()
        else:
            pl.when(cond_of)(own)

    loads = [
        pltpu.make_async_copy(h, v, load_sem.at[i])
        for i, (h, v) in enumerate(((rhs_h, rhs), (mask_h, mask), (xl_h, xl), (xu_h, xu)))
    ]
    for c in loads:
        c.start()

    barrier = pltpu.get_barrier_semaphore()
    for r in range(1, n_wall):
        pl.semaphore_signal(barrier, inc=1, device_id=(chord, lax.rem(wall + r, n_wall)),
                            device_id_type=pl.DeviceIdType.MESH)
    for r in range(1, n_chord):
        pl.semaphore_signal(barrier, inc=1, device_id=(lax.rem(chord + r, n_chord), wall),
                            device_id_type=pl.DeviceIdType.MESH)
    pl.semaphore_wait(barrier, n_wall + n_chord - 2)

    def to_wall(src, dst, send, recv, peer):
        return pltpu.make_async_remote_copy(
            src_ref=src, dst_ref=dst, send_sem=send, recv_sem=recv,
            device_id=(chord, peer), device_id_type=pl.DeviceIdType.MESH)

    for r in range(1, n_wall):
        peer = lax.rem(wall + r, n_wall)

        def send_eta(r=r, peer=peer):
            to_wall(el_h.at[:, peer], el.at[wall], el_send.at[r], el_recv.at[r], peer).start()
            to_wall(eu_h.at[:, peer], eu.at[wall], eu_send.at[r], eu_recv.at[r], peer).start()

        when(send_eta, peer < n_own)

    def own_eta():
        pltpu.make_async_copy(el_h.at[:, wall], el.at[wall], own_sem.at[0]).start()
        pltpu.make_async_copy(eu_h.at[:, wall], eu.at[wall], own_sem.at[1]).start()

    when(own_eta, wall < n_own)
    for c in loads:
        c.wait()

    lane = lax.broadcasted_iota(jnp.int32, (ROWS, width), 1)

    def chord_local(g, carry):
        at = pl.ds(pl.multiple_of(g * ROWS, ROWS), ROWS)
        hit = mask[at, :].astype(jnp.float32)
        source = jnp.stack([rhs[c, at, :] + hit * jet[c] for c in range(C)])[:, None]
        lower = scan_lanes(xl[:, at, :].reshape(C, C, ROWS, width), source, False)
        upper = scan_lanes(xu[:, at, :].reshape(C, C, ROWS, width), lower, True)
        prefix[:, at, :] = upper.reshape(C * 11, ROWS, width)
        packed = jnp.zeros((ROWS, width), jnp.float32)
        for a in range(C):
            for m in range(6):
                packed = jnp.where(lane == a * 6 + m, lower[a, m, :, width - 1 : width], packed)
            for m in range(11):
                packed = jnp.where(lane == 30 + a * 11 + m, upper[a, m, :, 0:1], packed)
        summary[chord, at, :] = packed
        return carry

    lax.fori_loop(0, groups, chord_local, 0)

    def to_chord(r, slot):
        return pltpu.make_async_remote_copy(
            src_ref=summary.at[slot], dst_ref=summary.at[slot],
            send_sem=chord_send.at[r], recv_sem=chord_recv.at[r],
            device_id=(lax.rem(chord + r, n_chord), wall), device_id_type=pl.DeviceIdType.MESH)

    for r in range(1, n_chord):
        to_chord(r, chord).start()
    for r in range(1, n_chord):
        to_chord(r, lax.rem(chord + n_chord - r, n_chord)).wait_recv()

    def chord_finish(g, carry):
        at = pl.ds(pl.multiple_of(g * ROWS, ROWS), ROWS)
        packs = [summary[d, at, :] for d in range(n_chord)]

        def field(d, i):
            return jnp.broadcast_to(packs[d][:, i : i + 1], (ROWS, width))

        zero = jnp.zeros((ROWS, width), jnp.float32)
        ins = [[zero] * C]
        for d in range(n_chord - 1):
            made = []
            for a in range(C):
                t = field(d, a * 6 + 5)
                if d > 0:
                    for b in range(C):
                        t = t + field(d, a * 6 + b) * ins[d][b]
                made.append(t)
            ins.append(made)
        backs = [None] * n_chord
        backs[n_chord - 1] = [zero] * C
        for d in range(n_chord - 1, 0, -1):
            made = []
            for a in range(C):
                base = 30 + a * 11
                t = field(d, base + 10)
                for b in range(C):
                    t = t + field(d, base + 5 + b) * ins[d][b]
                if d < n_chord - 1:
                    for b in range(C):
                        t = t + field(d, base + b) * backs[d][b]
                made.append(t)
            backs[d - 1] = made
        mine_in, mine_back = ins[0], backs[0]
        for d in range(1, n_chord):
            mine_in = [jnp.where(chord == d, x, y) for x, y in zip(ins[d], mine_in)]
            mine_back = [jnp.where(chord == d, x, y) for x, y in zip(backs[d], mine_back)]
        for a in range(C):
            t = prefix[a * 11 + 10, at, :]
            for b in range(C):
                t = t + prefix[a * 11 + 5 + b, at, :] * mine_in[b]
                t = t + prefix[a * 11 + b, at, :] * mine_back[b]
            for h in range(ROWS // rows_per_owner):
                sol[g * (ROWS // rows_per_owner) + h, a] = t[h * rows_per_owner : (h + 1) * rows_per_owner]
        return carry

    lax.fori_loop(0, groups, chord_finish, 0)

    for r in range(1, n_wall):
        peer = lax.rem(wall + r, n_wall)

        def send_sol(r=r, peer=peer):
            to_wall(sol.at[peer], sol_in.at[wall], sol_send.at[r], sol_recv.at[r], peer).start()

        when(send_sol, peer < n_own)

    def own_lines():
        own = pltpu.make_async_copy(sol.at[wall], sol_in.at[wall], own_sem.at[2])
        own.start()
        pltpu.make_async_copy(el_h.at[:, wall], el.at[wall], own_sem.at[0]).wait()
        pltpu.make_async_copy(eu_h.at[:, wall], eu.at[wall], own_sem.at[1]).wait()
        own.wait()
        for r in range(1, n_wall):
            source = lax.rem(wall + n_wall - r, n_wall)
            to_wall(el_h.at[:, 0], el.at[source], el_send.at[r], el_recv.at[r], source).wait_recv()
            to_wall(eu_h.at[:, 0], eu.at[source], eu_send.at[r], eu_recv.at[r], source).wait_recv()
            to_wall(sol.at[0], sol_in.at[source], sol_send.at[r], sol_recv.at[r], source).wait_recv()

        kind = flags_v[wall]
        factor = []
        for c in range(C):
            t = jnp.zeros(kind.shape, jnp.float32)
            for f in range(table.shape[0]):
                t = jnp.where(kind == f, table[f, c], t)
            factor.append(t)
        factor = jnp.stack(factor)

        def row(ref, d, j):
            return ref[d, :, pl.ds(j, kpo, stride=2), :]

        state = None
        lifted = []
        for d in range(n_wall):
            for j in range(2):
                value = row(sol_in, d, j)
                if state is None:
                    state = value * factor
                else:
                    blocks = row(el, d, j).reshape(C, C, kpo, width)
                    state = value + apply_blocks(blocks, state[:, None])[:, 0]
                lifted.append(state)
        state = None
        for d in range(n_wall - 1, -1, -1):
            for j in (1, 0):
                if state is None:
                    state = lifted[-1]
                else:
                    blocks = row(eu, d, j).reshape(C, C, kpo, width)
                    state = lifted[2 * d + j] + apply_blocks(blocks, state[:, None])[:, 0]
                res[d, :, pl.ds(j, kpo, stride=2), :] = state

        for r in range(1, n_wall):
            peer = lax.rem(wall + r, n_wall)
            to_wall(res.at[peer], out_h.at[:, wall], res_send.at[r], res_recv.at[r], peer).start()
        mine = pltpu.make_async_copy(res.at[wall], out_h.at[:, wall], own_sem.at[3])
        mine.start()
        mine.wait()
        for r in range(1, n_wall):
            peer = lax.rem(wall + r, n_wall)
            to_wall(res.at[peer], out_h.at[:, wall], res_send.at[r], res_recv.at[r], peer).wait_send()

    when(own_lines, wall < n_own)

    for r in range(1, n_wall):
        source = lax.rem(wall + n_wall - r, n_wall)
        peer = lax.rem(wall + r, n_wall)

        def take(r=r, source=source):
            to_wall(res.at[0], out_h.at[:, source], res_send.at[r], res_recv.at[r], source).wait_recv()

        def sent(r=r, peer=peer):
            to_wall(el_h.at[:, peer], el.at[wall], el_send.at[r], el_recv.at[r], peer).wait_send()
            to_wall(eu_h.at[:, peer], eu.at[wall], eu_send.at[r], eu_recv.at[r], peer).wait_send()
            to_wall(sol.at[peer], sol_in.at[wall], sol_send.at[r], sol_recv.at[r], peer).wait_send()

        when(take, source < n_own)
        when(sent, peer < n_own)
    for r in range(1, n_chord):
        to_chord(r, chord).wait_send()


def solution(mesh):
    n_chord, n_wall = mesh.shape["chord"], mesh.shape["wall"]

    def per_device(rhs, jet_mask, jet_source, wall_flags, bc_table,
                   xi_lower, xi_upper, eta_lower, eta_upper):
        comp, span, cells, width = rhs.shape
        n_own = min(n_wall, span)
        rows = span * cells
        rpo = rows // n_own
        flat = lambda x: x.reshape(comp * comp, rows, width)
        owned = lambda x: x.reshape(comp * comp, n_own, rpo, width)
        any_ = pl.BlockSpec(memory_space=pl.ANY)
        smem = pl.BlockSpec(memory_space=pltpu.SMEM)
        vmem = pl.BlockSpec(memory_space=pltpu.VMEM)
        f32 = jnp.float32
        dma = pltpu.SemaphoreType.DMA
        out = pl.pallas_call(
            functools.partial(kernel, n_chord, n_wall, n_own),
            out_shape=jax.ShapeDtypeStruct((comp, n_own, rpo, width), f32),
            in_specs=[any_, any_, smem, vmem, smem, any_, any_, any_, any_],
            out_specs=any_,
            scratch_shapes=[
                pltpu.VMEM((comp, rows, width), f32),
                pltpu.VMEM((rows, width), jnp.int32),
                pltpu.VMEM((comp * comp, rows, width), f32),
                pltpu.VMEM((comp * comp, rows, width), f32),
                pltpu.VMEM((n_wall, comp * comp, rpo, width), f32),
                pltpu.VMEM((n_wall, comp * comp, rpo, width), f32),
                pltpu.VMEM((comp * 11, rows, width), f32),
                pltpu.VMEM((n_chord, rows, width), f32),
                pltpu.VMEM((n_own, comp, rpo, width), f32),
                pltpu.VMEM((n_wall, comp, rpo, width), f32),
                pltpu.VMEM((n_wall, comp, rpo, width), f32),
                dma((4,)), dma((4,)), dma((n_chord,)), dma((n_chord,)),
                dma((n_wall,)), dma((n_wall,)), dma((n_wall,)), dma((n_wall,)),
                dma((n_wall,)), dma((n_wall,)), dma((n_wall,)), dma((n_wall,)),
            ],
            compiler_params=pltpu.CompilerParams(
                collective_id=0, has_side_effects=True, vmem_limit_bytes=48 * 1024 * 1024),
            name="sweeps",
        )(
            rhs.reshape(comp, rows, width), jet_mask.reshape(rows, width), jet_source,
            wall_flags.reshape(n_own, span // n_own, width), bc_table,
            flat(xi_lower), flat(xi_upper), owned(eta_lower), owned(eta_upper),
        )
        return out.reshape(comp, span, cells, width)

    placed = (
        P(None, None, "wall", "chord"),
        P(None, "wall", "chord"),
        P(),
        P(None, "chord"),
        P(),
        P(None, None, None, "wall", "chord"),
        P(None, None, None, "wall", "chord"),
        P(None, None, None, "wall", "chord"),
        P(None, None, None, "wall", "chord"),
    )
    return jax.shard_map(
        per_device, mesh=mesh, in_specs=placed,
        out_specs=P(None, None, "wall", "chord"), check_vma=False)
```

time: 438 us -> 39.5 us (0.09)
  local copies, waits for them, and re-layouts: 317 us -> 6.95 us
  blocking collectives: 35.2 us -> 0 us
  Pallas kernels: 0 us -> 32.1 us
  waiting for transfers between devices: 30.5 us -> 0 us
  other arithmetic: 21.8 us -> 0 us
  starting transfers between devices: 17 us -> 0 us
  between operations: 15.4 us -> 0.02 us
    slice x117 -> x0, local copies, waits for them, and re-layouts: 217 us -> none  [prefix_maps(): lax.associative_scan(compose, (blocks, values), axis=chain_axis)]
    pad x32 -> x0, local copies, waits for them, and re-layouts: 83.2 us -> none  [prefix_maps(): lax.associative_scan(compose, (blocks, values), axis=chain_axis)]
    all_gather x2 -> x0, blocking collectives: 35.2 us -> none  [carried_in(): gathered = jax.tree.map(lambda a: lax.all_gather(a, axis), part)]
    pallas_call x0 -> x1, Pallas kernels: none -> 32.1 us  [per_device(): pl.pallas_call(functools.partial(kernel, n_chord, n_wall, n_own), out_sha...]
    all_gather x2 -> x0, waiting for transfers between devices: 22.6 us -> none  [carried_in(): gathered = jax.tree.map(lambda a: lax.all_gather(a, axis), part)]
    all_to_all x4 -> x0, starting transfers between devices: 17 us -> none  [the longest x1 5.16 us: per_device(): lax.all_to_all(source, 'chord', split_axis=2, concat_axis=4, tiled=True)]
    reduce_sum x62 -> x0, other arithmetic: 12.7 us -> none  [block_product(): return jnp.sum(left[:, :, None] * right[None, :, :], axis=1)]
    all_to_all x4 -> x0, waiting for transfers between devices: 7.89 us -> none  [the longest x1 4.88 us: per_device(): lax.all_to_all(behind, 'chord', split_axis=4, concat_axis=2, tiled=True)]
  transfers between devices with their start and end apart: 6 -> 0, of which waited for: 4 -> 0; matrix products, arithmetic and copies ran while one was open for 37% -> 0% of each run, Pallas kernels for 0% -> 0%
where the time goes in v1:
time: 39.5 us; the launch traced here: 39.1 us
  Pallas kernels  32.1 us (81%)
  local copies, waits for them, and re-layouts  6.95 us (18%)
    pallas_call x1, Pallas kernels, per_device(): pl.pallas_call(functools.partial(kernel, n_chord, n_wall, n_own), out_sha...  32.1 us
    unnamed x19, local copies, waits for them, and re-layouts  6.95 us

profile of v1, /device:TPU:0, one launch (start us, length us, event | category | flops | bytes accessed | tf_op | source)
XLA Modules:
  0.0 39.1 jit_solution(11128124135986056441)
XLA Ops:
  0.0 0.0 copy-start.6
  0.0 0.0 copy-start.7
  0.0 0.0 copy-start.8
  0.0 0.7 %copy-done.6 = s32[16,128]{1,0:T(8,128)S(1)} copy-done((s32[16,128]{1,0:T(8,128)S(1)}, s32[16,128]{1,0:T(8,128)}, u32[]{:S(2)}) %copy-start.6) | copy-done | bytes 8216
  0.7 0.0 copy-done.7
  0.7 0.0 copy-done.8
  0.7 0.0 copy-start
  0.7 1.0 %copy-done = f32[5,5,16,2,128]{4,3,2,1,0:T(2,128)S(1)} copy-done((f32[5,5,16,2,128]{4,3,2,1,0:T(2,128)S(1)}, f32[5,5,16,2,128]{4,3,2,1,0:T(2,128)}, u32[]{:S(2)}) %copy-start) | copy-done | bytes 409624
  1.7 0.0 copy-start.1
  1.7 1.0 %copy-done.1 = f32[5,5,16,2,128]{4,3,2,1,0:T(2,128)S(1)} copy-done((f32[5,5,16,2,128]{4,3,2,1,0:T(2,128)S(1)}, f32[5,5,16,2,128]{4,3,2,1,0:T(2,128)}, u32[]{:S(2)}) %copy-start.1) | copy-done | bytes 409624
  2.7 0.0 copy-start.2
  2.7 1.0 %copy-done.2 = f32[5,5,16,2,128]{4,3,2,1,0:T(2,128)S(1)} copy-done((f32[5,5,16,2,128]{4,3,2,1,0:T(2,128)S(1)}, f32[5,5,16,2,128]{4,3,2,1,0:T(2,128)}, u32[]{:S(2)}) %copy-start.2) | copy-done | bytes 409624
  3.7 0.0 copy-start.3
  3.7 1.0 %copy-done.3 = f32[5,5,16,2,128]{4,3,2,1,0:T(2,128)S(1)} copy-done((f32[5,5,16,2,128]{4,3,2,1,0:T(2,128)S(1)}, f32[5,5,16,2,128]{4,3,2,1,0:T(2,128)}, u32[]{:S(2)}) %copy-start.3) | copy-done | bytes 409624
  4.7 0.0 copy-start.4
  4.7 0.9 %copy-done.4 = f32[5,16,2,128]{3,2,1,0:T(2,128)S(1)} copy-done((f32[5,16,2,128]{3,2,1,0:T(2,128)S(1)}, f32[5,16,2,128]{3,2,1,0:T(2,128)}, u32[]{:S(2)}) %copy-start.4) | copy-done | bytes 81944
  5.6 0.0 copy-start.5
  5.6 0.7 %copy-done.5 = s32[16,2,128]{2,1,0:T(2,128)S(1)} copy-done((s32[16,2,128]{2,1,0:T(2,128)S(1)}, s32[16,2,128]{2,1,0:T(2,128)}, u32[]{:S(2)}) %copy-start.5) | copy-done | bytes 16408
  6.3 32.1 %sweeps.1 = f32[5,8,4,128]{3,2,1,0:T(4,128)S(1)} custom-call(f32[5,32,128]{2,1,0:T(8,128)S(1)} %bitcast.13, s32[32,128]{1,0:T(8,128)S(1)} %bitcast.14, f32[5]{0:T(128)S(1)} %copy-done.8, s32[8,2,128]{2,1,0:T(2,128)S(1)} %bitcast.15, f32[3,5]{1,0:T(4,128)S(1)} %copy-done.7, f32[25,32,128]{2,1,0:T(8,128)S(1)} %bitcast.8, f32[25,32,128]{2,1,0:T(8,128)S(1)} %bitcast.9, ...), custom_call_target="tpu_custom_call" | custom-call | tf_op jit(solution)/shard_map/sweeps/pallas_call | solution.py:280
  38.4 0.6 %copy.11 = f32[5,16,2,128]{3,2,1,0:T(2,128)} copy(f32[5,16,2,128]{3,2,1,0:T(2,128)S(1)} %bitcast.12) | data formatting | bytes 163840
Async XLA Ops:
  0.0 0.7 %copy-start.6 = (s32[16,128]{1,0:T(8,128)S(1)}, s32[16,128]{1,0:T(8,128)}, u32[]{:S(2)}) copy-start(s32[16,128]{1,0:T(8,128)} %param.12) | copy-start | bytes 24580
  0.0 0.7 %copy-start.7 = (f32[3,5]{1,0:T(4,128)S(1)}, f32[3,5]{1,0:T(4,128)}, u32[]{:S(2)}) copy-start(f32[3,5]{1,0:T(4,128)} %table.1) | copy-start | bytes 184
  0.0 0.7 %copy-start.8 = (f32[5]{0:T(128)S(1)}, f32[5]{0:T(128)}, u32[]{:S(2)}) copy-start(f32[5]{0:T(128)} %jet.1) | copy-start | bytes 64
  0.7 1.0 %copy-start = (f32[5,5,16,2,128]{4,3,2,1,0:T(2,128)S(1)}, f32[5,5,16,2,128]{4,3,2,1,0:T(2,128)}, u32[]{:S(2)}) copy-start(f32[5,5,16,2,128]{4,3,2,1,0:T(2,128)} %param.14) | copy-start | bytes 1228804
  1.7 1.0 %copy-start.1 = (f32[5,5,16,2,128]{4,3,2,1,0:T(2,128)S(1)}, f32[5,5,16,2,128]{4,3,2,1,0:T(2,128)}, u32[]{:S(2)}) copy-start(f32[5,5,16,2,128]{4,3,2,1,0:T(2,128)} %param.15) | copy-start | bytes 1228804
  2.7 1.0 %copy-start.2 = (f32[5,5,16,2,128]{4,3,2,1,0:T(2,128)S(1)}, f32[5,5,16,2,128]{4,3,2,1,0:T(2,128)}, u32[]{:S(2)}) copy-start(f32[5,5,16,2,128]{4,3,2,1,0:T(2,128)} %param.16) | copy-start | bytes 1228804
  3.7 1.0 %copy-start.3 = (f32[5,5,16,2,128]{4,3,2,1,0:T(2,128)S(1)}, f32[5,5,16,2,128]{4,3,2,1,0:T(2,128)}, u32[]{:S(2)}) copy-start(f32[5,5,16,2,128]{4,3,2,1,0:T(2,128)} %param.17) | copy-start | bytes 1228804
  4.7 0.9 %copy-start.4 = (f32[5,16,2,128]{3,2,1,0:T(2,128)S(1)}, f32[5,16,2,128]{3,2,1,0:T(2,128)}, u32[]{:S(2)}) copy-start(f32[5,16,2,128]{3,2,1,0:T(2,128)} %param.9) | copy-start | bytes 245764
  5.6 0.7 %copy-start.5 = (s32[16,2,128]{2,1,0:T(2,128)S(1)}, s32[16,2,128]{2,1,0:T(2,128)}, u32[]{:S(2)}) copy-start(s32[16,2,128]{2,1,0:T(2,128)} %param.10) | copy-start | bytes 49156

commit v2 on v1

--- a/solution.py
+++ b/solution.py
@@ -43,9 +43,9 @@
 
 def kernel(
     n_chord, n_wall, n_own,
-    rhs_h, mask_h, jet, flags_v, table, xl_h, xu_h, el_h, eu_h,
+    rhs_h, mask_h, jet_h, flags_h, table_h, xl_h, xu_h, el_h, eu_h,
     out_h,
-    rhs, mask, xl, xu, el, eu, prefix, summary, sol, sol_in, res,
+    rhs, mask, xl, xu, jet, flags_v, table, el, eu, prefix, summary, sol, sol_in, res,
     load_sem, own_sem, chord_send, chord_recv, el_send, el_recv, eu_send, eu_recv,
     sol_send, sol_recv, res_send, res_recv,
 ):
@@ -64,7 +64,8 @@
 
     loads = [
         pltpu.make_async_copy(h, v, load_sem.at[i])
-        for i, (h, v) in enumerate(((rhs_h, rhs), (mask_h, mask), (xl_h, xl), (xu_h, xu)))
+        for i, (h, v) in enumerate(((xl_h, xl), (xu_h, xu), (rhs_h, rhs), (mask_h, mask),
+                                   (jet_h, jet), (flags_h, flags_v), (table_h, table)))
     ]
     for c in loads:
         c.start()
@@ -272,21 +273,22 @@
         rpo = rows // n_own
         flat = lambda x: x.reshape(comp * comp, rows, width)
         owned = lambda x: x.reshape(comp * comp, n_own, rpo, width)
-        any_ = pl.BlockSpec(memory_space=pl.ANY)
-        smem = pl.BlockSpec(memory_space=pltpu.SMEM)
-        vmem = pl.BlockSpec(memory_space=pltpu.VMEM)
+        hbm = pl.BlockSpec(memory_space=pltpu.HBM)
         f32 = jnp.float32
         dma = pltpu.SemaphoreType.DMA
         out = pl.pallas_call(
             functools.partial(kernel, n_chord, n_wall, n_own),
             out_shape=jax.ShapeDtypeStruct((comp, n_own, rpo, width), f32),
-            in_specs=[any_, any_, smem, vmem, smem, any_, any_, any_, any_],
-            out_specs=any_,
+            in_specs=[hbm] * 9,
+            out_specs=hbm,
             scratch_shapes=[
                 pltpu.VMEM((comp, rows, width), f32),
                 pltpu.VMEM((rows, width), jnp.int32),
                 pltpu.VMEM((comp * comp, rows, width), f32),
                 pltpu.VMEM((comp * comp, rows, width), f32),
+                pltpu.SMEM(jet_source.shape, f32),
+                pltpu.VMEM((n_own, span // n_own, width), jnp.int32),
+                pltpu.SMEM(bc_table.shape, f32),
                 pltpu.VMEM((n_wall, comp * comp, rpo, width), f32),
                 pltpu.VMEM((n_wall, comp * comp, rpo, width), f32),
                 pltpu.VMEM((comp * 11, rows, width), f32),
@@ -294,12 +296,12 @@
                 pltpu.VMEM((n_own, comp, rpo, width), f32),
                 pltpu.VMEM((n_wall, comp, rpo, width), f32),
                 pltpu.VMEM((n_wall, comp, rpo, width), f32),
-                dma((4,)), dma((4,)), dma((n_chord,)), dma((n_chord,)),
+                dma((7,)), dma((4,)), dma((n_chord,)), dma((n_chord,)),
                 dma((n_wall,)), dma((n_wall,)), dma((n_wall,)), dma((n_wall,)),
                 dma((n_wall,)), dma((n_wall,)), dma((n_wall,)), dma((n_wall,)),
             ],
             compiler_params=pltpu.CompilerParams(
-                collective_id=0, has_side_effects=True, vmem_limit_bytes=48 * 1024 * 1024),
+                collective_id=0, has_side_effects=True, vmem_limit_bytes=64 * 1024 * 1024),
             name="sweeps",
         )(
             rhs.reshape(comp, rows, width), jet_mask.reshape(rows, width), jet_source,

time: 39.5 us -> 33 us (0.84)
  local copies, waits for them, and re-layouts: 6.95 us -> 1.53 us
  Pallas kernels: 32.1 us -> 31.3 us
    unnamed x19 -> x1, local copies, waits for them, and re-layouts: 6.95 us -> 1.53 us
    pallas_call x1, Pallas kernels: 32.1 us -> 31.3 us  [per_device(): pl.pallas_call(functools.partial(kernel, n_chord, n_wall, n_own), out_sha...]
where the time goes in v2:
time: 33 us; the launch traced here: 32.8 us
  Pallas kernels  31.3 us (95%)
  local copies, waits for them, and re-layouts  1.53 us (5%)
    pallas_call x1, Pallas kernels, per_device(): pl.pallas_call(functools.partial(kernel, n_chord, n_wall, n_own), out_sha...  31.3 us
    unnamed x1, local copies, waits for them, and re-layouts  1.53 us

profile of v2, /device:TPU:0, one launch (start us, length us, event | category | flops | bytes accessed | tf_op | source)
XLA Modules:
  0.0 32.8 jit_solution(2572625236122337271)
XLA Ops:
  0.0 31.3 %sweeps.1 = f32[5,8,4,128]{3,2,1,0:T(4,128)} custom-call(f32[5,32,128]{2,1,0:T(8,128)} %bitcast.13, s32[32,128]{1,0:T(8,128)} %bitcast.14, f32[5]{0:T(128)} %jet_h.1, s32[8,2,128]{2,1,0:T(2,128)} %bitcast.15, f32[3,5]{1,0:T(4,128)} %table_h.1, f32[25,32,128]{2,1,0:T(8,128)} %bitcast.8, f32[25,32,128]{2,1,0:T(8,128)} %bitcast.9, f32[25,8,4,128]{3,2,1,0:T(4,128)} %bitcast.10, ...), custom_call_target="tpu_custom_call" | custom-call | tf_op jit(solution)/shard_map/sweeps/pallas_call | solution.py:279
  31.3 1.5 %copy.11 = f32[5,16,2,128]{3,2,1,0:T(2,128)} copy(f32[5,16,2,128]{3,2,1,0:T(2,128)} %bitcast.12) | data formatting | bytes 163840

commit v3 on v2

v3 whole, which is shorter than its diff:
```python
import functools

import jax
import jax.numpy as jnp
from jax import lax
from jax.experimental import pallas as pl
from jax.experimental.pallas import tpu as pltpu
from jax.sharding import PartitionSpec as P

C = 5
ROWS = 8


def shifted(x, step, fill_eye, reverse):
    a, m, rows, width = x.shape
    flat = x.reshape(a * m * rows, width)
    moved = pltpu.roll(flat, width - step if reverse else step, 1).reshape(x.shape)
    lane = lax.broadcasted_iota(jnp.int32, x.shape, 3)
    keep = lane < width - step if reverse else lane >= step
    row = lax.broadcasted_iota(jnp.int32, x.shape, 0)
    col = lax.broadcasted_iota(jnp.int32, x.shape, 1)
    fill = jnp.where(row == col, 1.0, 0.0).astype(jnp.float32)
    return jnp.where(keep, moved, fill)


def apply_blocks(left, right):
    total = left[:, 0:1] * right[0:1]
    for b in range(1, C):
        total = total + left[:, b : b + 1] * right[b : b + 1]
    return total


def scan_lanes(blocks, values, reverse):
    both = jnp.concatenate([blocks, values], axis=1)
    step = 1
    while step < both.shape[3]:
        moved = shifted(both, step, True, reverse)
        made = apply_blocks(both[:, :C], moved)
        both = jnp.concatenate([made[:, :C], made[:, C:] + both[:, C:]], axis=1)
        step *= 2
    return both


def kernel(
    n_chord, n_z, n_zo,
    rhs_h, mask_h, jet_h, flags_h, table_h, xl_h, xu_h, el_h, eu_h,
    out_h,
    rhs, mask, xl, xu, jet, flags_v, table, el, eu, prefix, summary, sol, sol_in, res,
    maps_out, maps_in, ends_out, ends_in, flow_out, flow_in, flow,
    load_sem, own_sem, chord_send, chord_recv, pair_send, pair_recv,
    maps_send, maps_recv, ends_send, ends_recv, flow_send, flow_recv,
):
    chord = lax.axis_index("chord")
    wall = lax.axis_index("wall")
    zi, core = wall // 2, lax.rem(wall, 2)
    other = 1 - core
    groups = rhs.shape[1] // ROWS
    half_groups = groups // 2
    lines = el.shape[2] // 2
    width = rhs.shape[2]
    kz = maps_out.shape[2]

    def when(own, cond_of):
        if n_zo == n_z:
            own()
        else:
            pl.when(cond_of)(own)

    loads = [
        pltpu.make_async_copy(h, v, load_sem.at[i])
        for i, (h, v) in enumerate(((xl_h, xl), (xu_h, xu), (rhs_h, rhs), (mask_h, mask),
                                   (jet_h, jet), (flags_h, flags_v), (table_h, table)))
    ]
    for c in loads:
        c.start()

    barrier = pltpu.get_barrier_semaphore()
    pl.semaphore_signal(barrier, inc=1, device_id=(chord, zi * 2 + other),
                        device_id_type=pl.DeviceIdType.MESH)
    for r in range(1, n_z):
        pl.semaphore_signal(barrier, inc=1, device_id=(chord, lax.rem(zi + r, n_z) * 2 + core),
                            device_id_type=pl.DeviceIdType.MESH)
    for r in range(1, n_chord):
        pl.semaphore_signal(barrier, inc=1, device_id=(lax.rem(chord + r, n_chord), wall),
                            device_id_type=pl.DeviceIdType.MESH)
    pl.semaphore_wait(barrier, n_z + n_chord - 1)

    def to_wall(src, dst, send, recv, peer):
        return pltpu.make_async_remote_copy(
            src_ref=src, dst_ref=dst, send_sem=send, recv_sem=recv,
            device_id=(chord, peer), device_id_type=pl.DeviceIdType.MESH)

    def to_core(i, src, dst):
        return to_wall(src, dst, pair_send.at[i], pair_recv.at[i], zi * 2 + other)

    def to_z(src, dst, send, recv, z):
        return to_wall(src, dst, send, recv, z * 2 + core)

    to_core(0, el_h.at[:, other], el.at[core]).start()
    to_core(1, eu_h.at[:, other], eu.at[core]).start()
    own_el = pltpu.make_async_copy(el_h.at[:, core], el.at[core], own_sem.at[0])
    own_eu = pltpu.make_async_copy(eu_h.at[:, core], eu.at[core], own_sem.at[1])
    own_el.start()
    own_eu.start()
    for c in loads:
        c.wait()

    def cell(ref, j):
        return ref[j // 2, :, pl.ds(j % 2, lines, stride=2), :]

    def block(ref, j):
        return cell(ref, j).reshape(C, C, lines, width)

    lane = lax.broadcasted_iota(jnp.int32, (ROWS, width), 1)

    def chord_local(g, carry):
        at = pl.ds(pl.multiple_of(g * ROWS, ROWS), ROWS)
        hit = mask[at, :].astype(jnp.float32)
        source = jnp.stack([rhs[c, at, :] + hit * jet[c] for c in range(C)])[:, None]
        lower = scan_lanes(xl[:, at, :].reshape(C, C, ROWS, width), source, False)
        upper = scan_lanes(xu[:, at, :].reshape(C, C, ROWS, width), lower, True)
        prefix[:, at, :] = upper.reshape(C * 11, ROWS, width)
        packed = jnp.zeros((ROWS, width), jnp.float32)
        for a in range(C):
            for m in range(6):
                packed = jnp.where(lane == a * 6 + m, lower[a, m, :, width - 1 : width], packed)
            for m in range(11):
                packed = jnp.where(lane == 30 + a * 11 + m, upper[a, m, :, 0:1], packed)
        summary[chord, at, :] = packed
        return carry

    lax.fori_loop(0, half_groups, chord_local, 0)

    own_el.wait()
    own_eu.wait()
    to_core(0, el_h.at[:, 0], el.at[other]).wait_recv()
    to_core(1, eu_h.at[:, 0], eu.at[other]).wait_recv()
    reach = [block(el, 0)]
    for j in range(1, 4):
        reach.append(apply_blocks(block(el, j), reach[-1]))
    back, through = reach[3], block(eu, 3)
    for j in (2, 1, 0):
        blocks = block(eu, j)
        back = apply_blocks(blocks, back) + reach[j]
        through = apply_blocks(blocks, through)
    for i, m in enumerate((reach[3], back, through)):
        m = m.reshape(C * C, lines, width)
        for o in range(n_zo):
            maps_out[o, i * 25 : (i + 1) * 25] = m[:, o * kz : (o + 1) * kz]

    def scatter(src, dst, send, recv):
        for r in range(1, n_z):
            z = lax.rem(zi + r, n_z)
            when(lambda r=r, z=z: to_z(src.at[z], dst.at[zi], send.at[r], recv.at[r], z).start(), z < n_zo)

    def scatter_own(src, dst, sem):
        return pltpu.make_async_copy(src.at[zi], dst.at[zi], sem)

    def scatter_sent(src, dst, send, recv):
        for r in range(1, n_z):
            z = lax.rem(zi + r, n_z)
            when(lambda r=r, z=z: to_z(src.at[z], dst.at[zi], send.at[r], recv.at[r], z).wait_send(), z < n_zo)

    def scattered(src, dst, send, recv):
        for r in range(1, n_z):
            z = lax.rem(zi + n_z - r, n_z)
            to_z(src.at[0], dst.at[z], send.at[r], recv.at[r], z).wait_recv()

    owner = zi < n_zo
    scatter(maps_out, maps_in, maps_send, maps_recv)
    when(lambda: scatter_own(maps_out, maps_in, own_sem.at[2]).start(), owner)
    lax.fori_loop(half_groups, groups, chord_local, 0)

    def to_chord(r, slot):
        return pltpu.make_async_remote_copy(
            src_ref=summary.at[slot], dst_ref=summary.at[slot],
            send_sem=chord_send.at[r], recv_sem=chord_recv.at[r],
            device_id=(lax.rem(chord + r, n_chord), wall), device_id_type=pl.DeviceIdType.MESH)

    for r in range(1, n_chord):
        to_chord(r, chord).start()
    for r in range(1, n_chord):
        to_chord(r, lax.rem(chord + n_chord - r, n_chord)).wait_recv()

    def chord_finish(g, carry):
        at = pl.ds(pl.multiple_of(g * ROWS, ROWS), ROWS)
        packs = [summary[d, at, :] for d in range(n_chord)]

        def field(d, i):
            return jnp.broadcast_to(packs[d][:, i : i + 1], (ROWS, width))

        zero = jnp.zeros((ROWS, width), jnp.float32)
        ins = [[zero] * C]
        for d in range(n_chord - 1):
            made = []
            for a in range(C):
                t = field(d, a * 6 + 5)
                if d > 0:
                    for b in range(C):
                        t = t + field(d, a * 6 + b) * ins[d][b]
                made.append(t)
            ins.append(made)
        backs = [None] * n_chord
        backs[n_chord - 1] = [zero] * C
        for d in range(n_chord - 1, 0, -1):
            made = []
            for a in range(C):
                base = 30 + a * 11
                t = field(d, base + 10)
                for b in range(C):
                    t = t + field(d, base + 5 + b) * ins[d][b]
                if d < n_chord - 1:
                    for b in range(C):
                        t = t + field(d, base + b) * backs[d][b]
                made.append(t)
            backs[d - 1] = made
        mine_in, mine_back = ins[0], backs[0]
        for d in range(1, n_chord):
            mine_in = [jnp.where(chord == d, x, y) for x, y in zip(ins[d], mine_in)]
            mine_back = [jnp.where(chord == d, x, y) for x, y in zip(backs[d], mine_back)]
        for a in range(C):
            t = prefix[a * 11 + 10, at, :]
            for b in range(C):
                t = t + prefix[a * 11 + 5 + b, at, :] * mine_in[b]
                t = t + prefix[a * 11 + b, at, :] * mine_back[b]
            sol[g // half_groups, a,
                pl.ds(pl.multiple_of(lax.rem(g, half_groups) * ROWS, ROWS), ROWS), :] = t
        return carry

    lax.fori_loop(0, groups, chord_finish, 0)

    to_core(2, sol.at[other], sol_in.at[core]).start()
    own_sol = pltpu.make_async_copy(sol.at[core], sol_in.at[core], own_sem.at[3])
    own_sol.start()
    kind = flags_v[core]
    factor = []
    for c in range(C):
        t = jnp.zeros(kind.shape, jnp.float32)
        for f in range(table.shape[0]):
            t = jnp.where(kind == f, table[f, c], t)
        factor.append(jnp.where(zi == 0, t, 1.0))
    factor = jnp.stack(factor)
    own_sol.wait()
    to_core(2, sol.at[0], sol_in.at[other]).wait_recv()

    def value(j):
        return cell(sol_in, j) * factor if j == 0 else cell(sol_in, j)

    def step(ref, j, state):
        return apply_blocks(block(ref, j), state[:, None])[:, 0]

    lifted = [value(0)]
    for j in range(1, 4):
        lifted.append(value(j) + step(el, j, lifted[-1]))
    first = lifted[3]
    for j in (2, 1, 0):
        first = lifted[j] + step(eu, j, first)
    for o in range(n_zo):
        ends_out[o, :C] = lifted[3][:, o * kz : (o + 1) * kz]
        ends_out[o, C:] = first[:, o * kz : (o + 1) * kz]
    scatter(ends_out, ends_in, ends_send, ends_recv)
    when(lambda: scatter_own(ends_out, ends_in, own_sem.at[4]).start(), owner)

    def own_lines():
        scatter_own(maps_out, maps_in, own_sem.at[2]).wait()
        scattered(maps_out, maps_in, maps_send, maps_recv)
        scatter_own(ends_out, ends_in, own_sem.at[4]).wait()
        scattered(ends_out, ends_in, ends_send, ends_recv)

        def through_map(z, i, state):
            m = maps_in[z, i * 25 : (i + 1) * 25].reshape(C, C, kz, width)
            return apply_blocks(m, state[:, None])[:, 0]

        zero = jnp.zeros((C, kz, width), jnp.float32)
        ins = [zero, ends_in[0, :C]]
        for z in range(1, n_z - 1):
            ins.append(ends_in[z, :C] + through_map(z, 0, ins[-1]))
        backs = [zero]
        for z in range(n_z - 1, 0, -1):
            t = ends_in[z, C:] + through_map(z, 1, ins[z])
            if z < n_z - 1:
                t = t + through_map(z, 2, backs[-1])
            backs.append(t)
        backs = backs[::-1]
        for z in range(n_z):
            flow_out[z, :C] = ins[z]
            flow_out[z, C:] = backs[z]
        for r in range(1, n_z):
            z = lax.rem(zi + r, n_z)
            to_z(flow_out.at[z], flow_in.at[zi], flow_send.at[r], flow_recv.at[r], z).start()
        scatter_own(flow_out, flow_in, own_sem.at[5]).start()

    when(own_lines, owner)
    when(lambda: scatter_own(flow_out, flow_in, own_sem.at[5]).wait(), owner)
    for r in range(1, n_z):
        z = lax.rem(zi + n_z - r, n_z)
        when(lambda r=r, z=z: to_z(flow_out.at[0], flow_in.at[z], flow_send.at[r], flow_recv.at[r], z).wait_recv(),
             z < n_zo)
    for o in range(n_zo):
        flow[:, o * kz : (o + 1) * kz] = flow_in[o]

    def ship(half):
        @pl.when(core == half)
        def _():
            pltpu.make_async_copy(res.at[half], out_h.at[:, half], own_sem.at[6]).start()

        @pl.when(core != half)
        def _():
            to_core(3, res.at[half], out_h.at[:, core]).start()

    state = flow[:C]
    lifted = []
    for j in range(4):
        state = value(j) + step(el, j, state)
        lifted.append(state)
    state = flow[C:]
    for j in (3, 2, 1, 0):
        state = lifted[j] + step(eu, j, state)
        res[j // 2, :, pl.ds(j % 2, lines, stride=2), :] = state
        if j % 2 == 0:
            ship(j // 2)

    for i, src, dst in ((0, el_h.at[:, other], el.at[core]), (1, eu_h.at[:, other], eu.at[core]),
                        (2, sol.at[other], sol_in.at[core]), (3, res.at[other], out_h.at[:, core])):
        to_core(i, src, dst).wait_send()
    scatter_sent(maps_out, maps_in, maps_send, maps_recv)
    scatter_sent(ends_out, ends_in, ends_send, ends_recv)

    def flow_sent():
        for r in range(1, n_z):
            z = lax.rem(zi + r, n_z)
            to_z(flow_out.at[z], flow_in.at[zi], flow_send.at[r], flow_recv.at[r], z).wait_send()

    when(flow_sent, owner)
    for r in range(1, n_chord):
        to_chord(r, chord).wait_send()
    pltpu.make_async_copy(res.at[core], out_h.at[:, core], own_sem.at[6]).wait()
    to_core(3, res.at[0], out_h.at[:, other]).wait_recv()


def solution(mesh):
    n_chord, n_wall = mesh.shape["chord"], mesh.shape["wall"]

    def per_device(rhs, jet_mask, jet_source, wall_flags, bc_table,
                   xi_lower, xi_upper, eta_lower, eta_upper):
        comp, span, cells, width = rhs.shape
        n_z = n_wall // 2
        lines = span // 2
        n_zo = min(n_z, lines)
        kz = lines // n_zo
        rows = span * cells
        half = rows // 2
        flat = lambda x: x.reshape(comp * comp, rows, width)
        halved = lambda x: x.reshape(comp * comp, 2, half, width)
        hbm = pl.BlockSpec(memory_space=pltpu.HBM)
        f32 = jnp.float32
        dma = pltpu.SemaphoreType.DMA
        out = pl.pallas_call(
            functools.partial(kernel, n_chord, n_z, n_zo),
            out_shape=jax.ShapeDtypeStruct((comp, 2, half, width), f32),
            in_specs=[hbm] * 9,
            out_specs=hbm,
            scratch_shapes=[
                pltpu.VMEM((comp, rows, width), f32),
                pltpu.VMEM((rows, width), jnp.int32),
                pltpu.VMEM((comp * comp, rows, width), f32),
                pltpu.VMEM((comp * comp, rows, width), f32),
                pltpu.SMEM(jet_source.shape, f32),
                pltpu.VMEM((2, lines, width), jnp.int32),
                pltpu.SMEM(bc_table.shape, f32),
                pltpu.VMEM((2, comp * comp, half, width), f32),
                pltpu.VMEM((2, comp * comp, half, width), f32),
                pltpu.VMEM((comp * 11, rows, width), f32),
                pltpu.VMEM((n_chord, rows, width), f32),
                pltpu.VMEM((2, comp, half, width), f32),
                pltpu.VMEM((2, comp, half, width), f32),
                pltpu.VMEM((2, comp, half, width), f32),
                pltpu.VMEM((n_zo, 3 * comp * comp, kz, width), f32),
                pltpu.VMEM((n_z, 3 * comp * comp, kz, width), f32),
                pltpu.VMEM((n_zo, 2 * comp, kz, width), f32),
                pltpu.VMEM((n_z, 2 * comp, kz, width), f32),
                pltpu.VMEM((n_z, 2 * comp, kz, width), f32),
                pltpu.VMEM((n_zo, 2 * comp, kz, width), f32),
                pltpu.VMEM((2 * comp, lines, width), f32),
                dma((7,)), dma((7,)), dma((n_chord,)), dma((n_chord,)), dma((4,)), dma((4,)),
                dma((n_z,)), dma((n_z,)), dma((n_z,)), dma((n_z,)), dma((n_z,)), dma((n_z,)),
            ],
            compiler_params=pltpu.CompilerParams(
                collective_id=0, has_side_effects=True, vmem_limit_bytes=64 * 1024 * 1024),
            name="sweeps",
        )(
            rhs.reshape(comp, rows, width), jet_mask.reshape(rows, width), jet_source,
            wall_flags.reshape(2, lines, width), bc_table,
            flat(xi_lower), flat(xi_upper), halved(eta_lower), halved(eta_upper),
        )
        return out.reshape(comp, span, cells, width)

    placed = (
        P(None, None, "wall", "chord"),
        P(None, "wall", "chord"),
        P(),
        P(None, "chord"),
        P(),
        P(None, None, None, "wall", "chord"),
        P(None, None, None, "wall", "chord"),
        P(None, None, None, "wall", "chord"),
        P(None, None, None, "wall", "chord"),
    )
    return jax.shard_map(
        per_device, mesh=mesh, in_specs=placed,
        out_specs=P(None, None, "wall", "chord"), check_vma=False)
```

time: 33 us -> 28.8 us (0.87)
  Pallas kernels: 31.3 us -> 27.1 us
    pallas_call x1, Pallas kernels: 31.3 us -> 27.1 us  [per_device(): pl.pallas_call(functools.partial(kernel, n_chord, n_z, n_zo), out_shape=j...]
where the time goes in v3:
time: 28.8 us; the launch traced here: 28.6 us
  Pallas kernels  27.1 us (94%)
  local copies, waits for them, and re-layouts  1.53 us (5%)
    pallas_call x1, Pallas kernels, per_device(): pl.pallas_call(functools.partial(kernel, n_chord, n_z, n_zo), out_shape=j...  27.1 us
    unnamed x1, local copies, waits for them, and re-layouts  1.53 us

profile of v3, /device:TPU:0, one launch (start us, length us, event | category | flops | bytes accessed | tf_op | source)
XLA Modules:
  0.0 28.6 jit_solution(9009582989990571171)
XLA Ops:
  0.0 27.1 %sweeps.1 = f32[5,2,16,128]{3,2,1,0:T(8,128)} custom-call(f32[5,32,128]{2,1,0:T(8,128)} %bitcast.13, s32[32,128]{1,0:T(8,128)} %bitcast.14, f32[5]{0:T(128)} %jet_h.1, s32[2,8,128]{2,1,0:T(8,128)} %bitcast.15, f32[3,5]{1,0:T(4,128)} %table_h.1, f32[25,32,128]{2,1,0:T(8,128)} %bitcast.8, f32[25,32,128]{2,1,0:T(8,128)} %bitcast.9, ...), custom_call_target="tpu_custom_call" | custom-call | tf_op jit(solution)/shard_map/sweeps/pallas_call | solution.py:358
  27.1 1.5 %copy.11 = f32[5,16,2,128]{3,2,1,0:T(2,128)} copy(f32[5,16,2,128]{3,2,1,0:T(2,128)} %bitcast.12) | data formatting | bytes 163840

commit v4 on v3

--- a/solution.py
+++ b/solution.py
@@ -9,6 +9,7 @@
 
 C = 5
 ROWS = 8
+PACK = 4
 
 
 def shifted(x, step, fill_eye, reverse):
@@ -30,15 +31,36 @@
     return total
 
 
-def scan_lanes(blocks, values, reverse):
-    both = jnp.concatenate([blocks, values], axis=1)
-    step = 1
+def compose(later, earlier):
+    made = apply_blocks(later[:, :C], earlier)
+    return jnp.concatenate([made[:, :C], made[:, C:] + later[:, C:]], axis=1)
+
+
+def scan_lanes(both, reverse):
+    step = PACK
     while step < both.shape[3]:
-        moved = shifted(both, step, True, reverse)
-        made = apply_blocks(both[:, :C], moved)
-        both = jnp.concatenate([made[:, :C], made[:, C:] + both[:, C:]], axis=1)
+        both = compose(both, shifted(both, step, True, reverse))
         step *= 2
     return both
+
+
+def roll2(x, by):
+    width = x.shape[-1]
+    return pltpu.roll(x.reshape(-1, width), by % width, 1).reshape(x.shape)
+
+
+def interleave(parts):
+    lane = lax.broadcasted_iota(jnp.int32, parts[0].shape, 2)
+    for bit in (1, 2):
+        odd = (lane & bit) != 0
+        made = list(parts)
+        for i in range(PACK):
+            if i & bit == 0:
+                lo, hi = parts[i], parts[i | bit]
+                made[i] = jnp.where(odd, roll2(hi, bit), lo)
+                made[i | bit] = jnp.where(odd, hi, roll2(lo, -bit))
+        parts = made
+    return parts
 
 
 def kernel(
@@ -113,23 +135,51 @@
 
     lane = lax.broadcasted_iota(jnp.int32, (ROWS, width), 1)
 
-    def chord_local(g, carry):
-        at = pl.ds(pl.multiple_of(g * ROWS, ROWS), ROWS)
-        hit = mask[at, :].astype(jnp.float32)
-        source = jnp.stack([rhs[c, at, :] + hit * jet[c] for c in range(C)])[:, None]
-        lower = scan_lanes(xl[:, at, :].reshape(C, C, ROWS, width), source, False)
-        upper = scan_lanes(xu[:, at, :].reshape(C, C, ROWS, width), lower, True)
-        prefix[:, at, :] = upper.reshape(C * 11, ROWS, width)
-        packed = jnp.zeros((ROWS, width), jnp.float32)
-        for a in range(C):
-            for m in range(6):
-                packed = jnp.where(lane == a * 6 + m, lower[a, m, :, width - 1 : width], packed)
-            for m in range(11):
-                packed = jnp.where(lane == 30 + a * 11 + m, upper[a, m, :, 0:1], packed)
-        summary[chord, at, :] = packed
-        return carry
-
-    lax.fori_loop(0, half_groups, chord_local, 0)
+    def tile(ref, q):
+        return ref[:, q * ROWS : (q + 1) * ROWS, :]
+
+    def sources(q):
+        hit = mask[q * ROWS : (q + 1) * ROWS, :].astype(jnp.float32)
+        x = tile(rhs, q)
+        return jnp.stack([x[c] + hit * jet[c] for c in range(C)])
+
+    source = interleave([sources(q) for q in range(PACK)])
+    lower = interleave([tile(xl, q) for q in range(PACK)])
+    runs = []
+    for t in range(PACK):
+        x = jnp.concatenate([lower[t].reshape(C, C, ROWS, width), source[t][:, None]], axis=1)
+        runs.append(compose(x, runs[-1]) if runs else x)
+    last = scan_lanes(runs[PACK - 1], False)
+    before = shifted(last, PACK, True, False)
+    full = [compose(runs[t], before) for t in range(PACK - 1)] + [last]
+    upper = interleave([tile(xu, q) for q in range(PACK)])
+    runs = [None] * PACK
+    for t in range(PACK - 1, -1, -1):
+        x = jnp.concatenate([upper[t].reshape(C, C, ROWS, width), full[t]], axis=1)
+        runs[t] = compose(x, runs[t + 1]) if t < PACK - 1 else x
+    first = scan_lanes(runs[0], True)
+    before = shifted(first, PACK, True, True)
+    packs = [jnp.zeros((ROWS, width), jnp.float32) for _ in range(summary.shape[1])]
+    fields = [(last[a, m], PACK - width) for a in range(C) for m in range(6)]
+    fields += [(first[a, m], 0) for a in range(C) for m in range(11)]
+    per = width // PACK
+    for i, (x, base) in enumerate(fields):
+        at = PACK * (i % per)
+        packs[i // per] = jnp.where((lane >= at) & (lane < at + PACK), roll2(x, at + base), packs[i // per])
+    for i, x in enumerate(packs):
+        summary[chord, i] = x
+
+    def to_chord(r, slot):
+        return pltpu.make_async_remote_copy(
+            src_ref=summary.at[slot], dst_ref=summary.at[slot],
+            send_sem=chord_send.at[r], recv_sem=chord_recv.at[r],
+            device_id=(lax.rem(chord + r, n_chord), wall), device_id_type=pl.DeviceIdType.MESH)
+
+    for r in range(1, n_chord):
+        to_chord(r, chord).start()
+    prefix[0] = first.reshape(C * 11, ROWS, width)
+    for t in range(1, PACK):
+        prefix[t] = compose(runs[t], before).reshape(C * 11, ROWS, width)
 
     own_el.wait()
     own_eu.wait()
@@ -169,65 +219,57 @@
     owner = zi < n_zo
     scatter(maps_out, maps_in, maps_send, maps_recv)
     when(lambda: scatter_own(maps_out, maps_in, own_sem.at[2]).start(), owner)
-    lax.fori_loop(half_groups, groups, chord_local, 0)
-
-    def to_chord(r, slot):
-        return pltpu.make_async_remote_copy(
-            src_ref=summary.at[slot], dst_ref=summary.at[slot],
-            send_sem=chord_send.at[r], recv_sem=chord_recv.at[r],
-            device_id=(lax.rem(chord + r, n_chord), wall), device_id_type=pl.DeviceIdType.MESH)
-
-    for r in range(1, n_chord):
-        to_chord(r, chord).start()
     for r in range(1, n_chord):
         to_chord(r, lax.rem(chord + n_chord - r, n_chord)).wait_recv()
 
-    def chord_finish(g, carry):
-        at = pl.ds(pl.multiple_of(g * ROWS, ROWS), ROWS)
-        packs = [summary[d, at, :] for d in range(n_chord)]
-
-        def field(d, i):
-            return jnp.broadcast_to(packs[d][:, i : i + 1], (ROWS, width))
-
-        zero = jnp.zeros((ROWS, width), jnp.float32)
-        ins = [[zero] * C]
-        for d in range(n_chord - 1):
-            made = []
-            for a in range(C):
-                t = field(d, a * 6 + 5)
-                if d > 0:
-                    for b in range(C):
-                        t = t + field(d, a * 6 + b) * ins[d][b]
-                made.append(t)
-            ins.append(made)
-        backs = [None] * n_chord
-        backs[n_chord - 1] = [zero] * C
-        for d in range(n_chord - 1, 0, -1):
-            made = []
-            for a in range(C):
-                base = 30 + a * 11
-                t = field(d, base + 10)
+
+    def field(d, i):
+        return roll2(summary[d, i // per], -PACK * (i % per))
+
+    zero = jnp.zeros((ROWS, width), jnp.float32)
+    ins = [[zero] * C]
+    for d in range(n_chord - 1):
+        made = []
+        for a in range(C):
+            t = field(d, a * 6 + 5)
+            if d > 0:
                 for b in range(C):
-                    t = t + field(d, base + 5 + b) * ins[d][b]
-                if d < n_chord - 1:
-                    for b in range(C):
-                        t = t + field(d, base + b) * backs[d][b]
-                made.append(t)
-            backs[d - 1] = made
-        mine_in, mine_back = ins[0], backs[0]
-        for d in range(1, n_chord):
-            mine_in = [jnp.where(chord == d, x, y) for x, y in zip(ins[d], mine_in)]
-            mine_back = [jnp.where(chord == d, x, y) for x, y in zip(backs[d], mine_back)]
+                    t = t + field(d, a * 6 + b) * ins[d][b]
+            made.append(t)
+        ins.append(made)
+    backs = [None] * n_chord
+    backs[n_chord - 1] = [zero] * C
+    for d in range(n_chord - 1, 0, -1):
+        made = []
         for a in range(C):
-            t = prefix[a * 11 + 10, at, :]
+            base = 30 + a * 11
+            t = field(d, base + 10)
             for b in range(C):
-                t = t + prefix[a * 11 + 5 + b, at, :] * mine_in[b]
-                t = t + prefix[a * 11 + b, at, :] * mine_back[b]
-            sol[g // half_groups, a,
-                pl.ds(pl.multiple_of(lax.rem(g, half_groups) * ROWS, ROWS), ROWS), :] = t
-        return carry
-
-    lax.fori_loop(0, groups, chord_finish, 0)
+                t = t + field(d, base + 5 + b) * ins[d][b]
+            if d < n_chord - 1:
+                for b in range(C):
+                    t = t + field(d, base + b) * backs[d][b]
+            made.append(t)
+        backs[d - 1] = made
+    mine_in, mine_back = ins[0], backs[0]
+    for d in range(1, n_chord):
+        mine_in = [jnp.where(chord == d, x, y) for x, y in zip(ins[d], mine_in)]
+        mine_back = [jnp.where(chord == d, x, y) for x, y in zip(backs[d], mine_back)]
+    inflow = jnp.where(lane[None] < PACK, jnp.stack(mine_in + mine_back), 0.0)
+    by = PACK
+    while by < width:
+        inflow = inflow + roll2(inflow, by)
+        by *= 2
+    behind = []
+    for t in range(PACK):
+        x = prefix[t].reshape(C, 11, ROWS, width)
+        total = x[:, 10]
+        for b in range(C):
+            total = total + x[:, 5 + b] * inflow[b] + x[:, b] * inflow[C + b]
+        behind.append(total)
+    for q, x in enumerate(interleave(behind)):
+        at = (q % half_groups) * ROWS
+        sol[q // half_groups, :, at : at + ROWS, :] = x
 
     to_core(2, sol.at[other], sol_in.at[core]).start()
     own_sol = pltpu.make_async_copy(sol.at[core], sol_in.at[core], own_sem.at[3])
@@ -370,8 +412,8 @@
                 pltpu.SMEM(bc_table.shape, f32),
                 pltpu.VMEM((2, comp * comp, half, width), f32),
                 pltpu.VMEM((2, comp * comp, half, width), f32),
-                pltpu.VMEM((comp * 11, rows, width), f32),
-                pltpu.VMEM((n_chord, rows, width), f32),
+                pltpu.VMEM((PACK, comp * 11, ROWS, width), f32),
+                pltpu.VMEM((n_chord, -(-85 * PACK // width), ROWS, width), f32),
                 pltpu.VMEM((2, comp, half, width), f32),
                 pltpu.VMEM((2, comp, half, width), f32),
                 pltpu.VMEM((2, comp, half, width), f32),

time: 28.8 us -> 23.5 us (0.82)
  Pallas kernels: 27.1 us -> 21.8 us
    pallas_call x1, Pallas kernels: 27.1 us -> 21.8 us  [per_device(): pl.pallas_call(functools.partial(kernel, n_chord, n_z, n_zo), out_shape=j...]
where the time goes in v4:
time: 23.5 us; the launch traced here: 23.4 us
  Pallas kernels  21.8 us (93%)
  local copies, waits for them, and re-layouts  1.53 us (7%)
    pallas_call x1, Pallas kernels, per_device(): pl.pallas_call(functools.partial(kernel, n_chord, n_z, n_zo), out_shape=j...  21.8 us
    unnamed x1, local copies, waits for them, and re-layouts  1.53 us

profile of v4, /device:TPU:0, one launch (start us, length us, event | category | flops | bytes accessed | tf_op | source)
XLA Modules:
  0.0 23.4 jit_solution(14935181635275056052)
XLA Ops:
  0.0 21.8 %sweeps.1 = f32[5,2,16,128]{3,2,1,0:T(8,128)} custom-call(f32[5,32,128]{2,1,0:T(8,128)} %bitcast.13, s32[32,128]{1,0:T(8,128)} %bitcast.14, f32[5]{0:T(128)} %jet_h.1, s32[2,8,128]{2,1,0:T(8,128)} %bitcast.15, f32[3,5]{1,0:T(4,128)} %table_h.1, f32[25,32,128]{2,1,0:T(8,128)} %bitcast.8, f32[25,32,128]{2,1,0:T(8,128)} %bitcast.9, ...), custom_call_target="tpu_custom_call" | custom-call | tf_op jit(solution)/shard_map/sweeps/pallas_call | solution.py:400
  21.8 1.5 %copy.11 = f32[5,16,2,128]{3,2,1,0:T(2,128)} copy(f32[5,16,2,128]{3,2,1,0:T(2,128)} %bitcast.12) | data formatting | bytes 163840

commit v5 on v4

--- a/solution.py
+++ b/solution.py
@@ -124,8 +124,8 @@
     own_eu = pltpu.make_async_copy(eu_h.at[:, core], eu.at[core], own_sem.at[1])
     own_el.start()
     own_eu.start()
-    for c in loads:
-        c.wait()
+    for i in (0, 2, 3, 4):
+        loads[i].wait()
 
     def cell(ref, j):
         return ref[j // 2, :, pl.ds(j % 2, lines, stride=2), :]
@@ -152,6 +152,7 @@
     last = scan_lanes(runs[PACK - 1], False)
     before = shifted(last, PACK, True, False)
     full = [compose(runs[t], before) for t in range(PACK - 1)] + [last]
+    loads[1].wait()
     upper = interleave([tile(xu, q) for q in range(PACK)])
     runs = [None] * PACK
     for t in range(PACK - 1, -1, -1):
@@ -193,7 +194,7 @@
         blocks = block(eu, j)
         back = apply_blocks(blocks, back) + reach[j]
         through = apply_blocks(blocks, through)
-    for i, m in enumerate((reach[3], back, through)):
+    for i, m in enumerate((back, reach[3], through)):
         m = m.reshape(C * C, lines, width)
         for o in range(n_zo):
             maps_out[o, i * 25 : (i + 1) * 25] = m[:, o * kz : (o + 1) * kz]
@@ -217,7 +218,25 @@
             to_z(src.at[0], dst.at[z], send.at[r], recv.at[r], z).wait_recv()
 
     owner = zi < n_zo
-    scatter(maps_out, maps_in, maps_send, maps_recv)
+    def map_copies(z_out, z_in, r, to):
+        return [
+            to_z(maps_out.at[z_out, part], maps_in.at[z_in, part], maps_send.at[i, r], maps_recv.at[i, r], to)
+            for i, part in enumerate((pl.ds(0, C * C), pl.ds(C * C, 2 * C * C)))
+        ]
+
+    def each_map(act, copies, sender, condition):
+        turn, inner = sender > 0, (sender > 0) & (sender < n_z - 1)
+        if condition is not None:
+            turn, inner = turn & condition, inner & condition
+        pl.when(turn)(lambda: act(copies[0]))
+        pl.when(inner)(lambda: act(copies[1]))
+
+    def maps_outward(act):
+        for r in range(1, n_z):
+            z = lax.rem(zi + r, n_z)
+            each_map(act, map_copies(z, zi, r, z), zi, None if n_zo == n_z else z < n_zo)
+
+    maps_outward(lambda c: c.start())
     when(lambda: scatter_own(maps_out, maps_in, own_sem.at[2]).start(), owner)
     for r in range(1, n_chord):
         to_chord(r, lax.rem(chord + n_chord - r, n_chord)).wait_recv()
@@ -274,6 +293,8 @@
     to_core(2, sol.at[other], sol_in.at[core]).start()
     own_sol = pltpu.make_async_copy(sol.at[core], sol_in.at[core], own_sem.at[3])
     own_sol.start()
+    loads[5].wait()
+    loads[6].wait()
     kind = flags_v[core]
     factor = []
     for c in range(C):
@@ -305,7 +326,9 @@
 
     def own_lines():
         scatter_own(maps_out, maps_in, own_sem.at[2]).wait()
-        scattered(maps_out, maps_in, maps_send, maps_recv)
+        for r in range(1, n_z):
+            z = lax.rem(zi + n_z - r, n_z)
+            each_map(lambda c: c.wait_recv(), map_copies(0, z, r, z), z, None)
         scatter_own(ends_out, ends_in, own_sem.at[4]).wait()
         scattered(ends_out, ends_in, ends_send, ends_recv)
 
@@ -316,10 +339,10 @@
         zero = jnp.zeros((C, kz, width), jnp.float32)
         ins = [zero, ends_in[0, :C]]
         for z in range(1, n_z - 1):
-            ins.append(ends_in[z, :C] + through_map(z, 0, ins[-1]))
+            ins.append(ends_in[z, :C] + through_map(z, 1, ins[-1]))
         backs = [zero]
         for z in range(n_z - 1, 0, -1):
-            t = ends_in[z, C:] + through_map(z, 1, ins[z])
+            t = ends_in[z, C:] + through_map(z, 0, ins[z])
             if z < n_z - 1:
                 t = t + through_map(z, 2, backs[-1])
             backs.append(t)
@@ -365,7 +388,7 @@
     for i, src, dst in ((0, el_h.at[:, other], el.at[core]), (1, eu_h.at[:, other], eu.at[core]),
                         (2, sol.at[other], sol_in.at[core]), (3, res.at[other], out_h.at[:, core])):
         to_core(i, src, dst).wait_send()
-    scatter_sent(maps_out, maps_in, maps_send, maps_recv)
+    maps_outward(lambda c: c.wait_send())
     scatter_sent(ends_out, ends_in, ends_send, ends_recv)
 
     def flow_sent():
@@ -425,7 +448,7 @@
                 pltpu.VMEM((n_zo, 2 * comp, kz, width), f32),
                 pltpu.VMEM((2 * comp, lines, width), f32),
                 dma((7,)), dma((7,)), dma((n_chord,)), dma((n_chord,)), dma((4,)), dma((4,)),
-                dma((n_z,)), dma((n_z,)), dma((n_z,)), dma((n_z,)), dma((n_z,)), dma((n_z,)),
+                dma((2, n_z)), dma((2, n_z)), dma((n_z,)), dma((n_z,)), dma((n_z,)), dma((n_z,)),
             ],
             compiler_params=pltpu.CompilerParams(
                 collective_id=0, has_side_effects=True, vmem_limit_bytes=64 * 1024 * 1024),

time: 23.5 us -> 23.3 us (level)
  no operation moved by 1% of the time
where the time goes in v5:
time: 23.3 us; the launch traced here: 23.2 us
  Pallas kernels  21.6 us (93%)
  local copies, waits for them, and re-layouts  1.53 us (7%)
    pallas_call x1, Pallas kernels, per_device(): pl.pallas_call(functools.partial(kernel, n_chord, n_z, n_zo), out_shape=j...  21.6 us
    unnamed x1, local copies, waits for them, and re-layouts  1.53 us

profile of v5, /device:TPU:0, one launch (start us, length us, event | category | flops | bytes accessed | tf_op | source)
XLA Modules:
  0.0 23.2 jit_solution(5421973846931348536)
XLA Ops:
  0.0 21.6 %sweeps.1 = f32[5,2,16,128]{3,2,1,0:T(8,128)} custom-call(f32[5,32,128]{2,1,0:T(8,128)} %bitcast.13, s32[32,128]{1,0:T(8,128)} %bitcast.14, f32[5]{0:T(128)} %jet_h.1, s32[2,8,128]{2,1,0:T(8,128)} %bitcast.15, f32[3,5]{1,0:T(4,128)} %table_h.1, f32[25,32,128]{2,1,0:T(8,128)} %bitcast.8, f32[25,32,128]{2,1,0:T(8,128)} %bitcast.9, ...), custom_call_target="tpu_custom_call" | custom-call | tf_op jit(solution)/shard_map/sweeps/pallas_call | solution.py:423
  21.6 1.5 %copy.11 = f32[5,16,2,128]{3,2,1,0:T(2,128)} copy(f32[5,16,2,128]{3,2,1,0:T(2,128)} %bitcast.12) | data formatting | bytes 163840

commit v6 on v5

--- a/solution.py
+++ b/solution.py
@@ -178,9 +178,6 @@
 
     for r in range(1, n_chord):
         to_chord(r, chord).start()
-    prefix[0] = first.reshape(C * 11, ROWS, width)
-    for t in range(1, PACK):
-        prefix[t] = compose(runs[t], before).reshape(C * 11, ROWS, width)
 
     own_el.wait()
     own_eu.wait()
@@ -238,6 +235,9 @@
 
     maps_outward(lambda c: c.start())
     when(lambda: scatter_own(maps_out, maps_in, own_sem.at[2]).start(), owner)
+    prefix[0] = first.reshape(C * 11, ROWS, width)
+    for t in range(1, PACK):
+        prefix[t] = compose(runs[t], before).reshape(C * 11, ROWS, width)
     for r in range(1, n_chord):
         to_chord(r, lax.rem(chord + n_chord - r, n_chord)).wait_recv()
 

time: 23.3 us -> 23.2 us (level)
  no operation moved by 1% of the time
where the time goes in v6:
time: 23.2 us; the launch traced here: 23 us
  Pallas kernels  21.5 us (93%)
  local copies, waits for them, and re-layouts  1.53 us (7%)
    pallas_call x1, Pallas kernels, per_device(): pl.pallas_call(functools.partial(kernel, n_chord, n_z, n_zo), out_shape=j...  21.5 us
    unnamed x1, local copies, waits for them, and re-layouts  1.53 us

profile of v6, /device:TPU:0, one launch (start us, length us, event | category | flops | bytes accessed | tf_op | source)
XLA Modules:
  0.0 23.0 jit_solution(12801152580551288795)
XLA Ops:
  0.0 21.5 %sweeps.1 = f32[5,2,16,128]{3,2,1,0:T(8,128)} custom-call(f32[5,32,128]{2,1,0:T(8,128)} %bitcast.13, s32[32,128]{1,0:T(8,128)} %bitcast.14, f32[5]{0:T(128)} %jet_h.1, s32[2,8,128]{2,1,0:T(8,128)} %bitcast.15, f32[3,5]{1,0:T(4,128)} %table_h.1, f32[25,32,128]{2,1,0:T(8,128)} %bitcast.8, f32[25,32,128]{2,1,0:T(8,128)} %bitcast.9, ...), custom_call_target="tpu_custom_call" | custom-call | tf_op jit(solution)/shard_map/sweeps/pallas_call | solution.py:423
  21.5 1.5 %copy.11 = f32[5,16,2,128]{3,2,1,0:T(2,128)} copy(f32[5,16,2,128]{3,2,1,0:T(2,128)} %bitcast.12) | data formatting | bytes 163840
